TPU v7x, 32 devices: a whole 2x2x4 slice. The times are simulated.
32 devices in a mesh: line: 4 (over y, x), plane: 8 (over z, core).
Axes of the slice: x: 2, y: 2, z: 4, core: 2. Of those that a mesh axis runs over, the one named last changes fastest.
Arguments:
- flux_x: float32 [256, 5, 8192], P('line', None, 'plane'), may hold values from -1600 to 1600
- flux_z: float32 [256, 5, 8192], P('line', None, 'plane'), may hold values from -1600 to 1600
- viscous: float32 [256, 8192], P('line', 'plane'), may hold values from 4000 to 16000
- jacobian: float32 [256, 5, 5, 8192], P('line', None, None, 'plane'), may hold values from -10 to 10
Outputs:
- delta: float32 [256, 5, 8192], P('line', None, 'plane')
All inputs are finite; a program needn't handle non-finite values.
Results may differ from a plain program's by a relative error of at most 0.0003.
Values sent between devices are 32-bit elements; how exact they have to be, the bound alone decides.
A program may use at most 192 MiB of HBM per device.

v0:
```python
import jax
import jax.numpy as jnp
from jax import lax
from jax.sharding import PartitionSpec as P

courant = 10.0


def padded(block, sides, width):
    for axis, dim in sides:
        count = lax.axis_size(axis)
        forward = [(i, i + 1) for i in range(count - 1)]
        backward = [(target, source) for source, target in forward]
        low = lax.ppermute(
            lax.slice_in_dim(block, block.shape[dim] - width, None, axis=dim), axis, forward
        )
        high = lax.ppermute(lax.slice_in_dim(block, 0, width, axis=dim), axis, backward)
        block = jnp.concatenate([low, block, high], axis=dim)
    return block


def from_behind(block, axis, distance):
    devices = range(lax.axis_size(axis))
    route = [(i - distance, i) for i in devices if i - distance in devices]
    return lax.ppermute(block, axis, route)


def combine_blocks(matrix, operand):
    return jnp.sum(matrix[:, :, None, :] * operand[None, :, :, :], axis=1)


def solve_small(matrix, columns):
    extent = matrix.shape[0]
    for column in range(extent):
        inverse = 1.0 / matrix[column, column]
        pivot_row = matrix[column] * inverse
        column_row = columns[column] * inverse
        factor = matrix[:, column]
        matrix = matrix - factor[:, None, :] * pivot_row[None]
        columns = columns - factor[:, None, :] * column_row[None]
        matrix = matrix.at[column].set(pivot_row)
        columns = columns.at[column].set(column_row)
    return columns


def cell_blocks(viscous, jacobian):
    identity = jnp.eye(5, dtype=jnp.float32)[:, :, None]
    spread = viscous[None, None, :]
    lower_block = -spread * identity - jacobian
    center_block = (1.0 + 2.0 * spread) * identity
    upper_block = -spread * identity + jacobian
    return (lower_block, center_block, upper_block)


def eliminate(previous, lower_block, center_block, upper_block, source):
    extent = center_block.shape[0]
    schur = center_block - combine_blocks(lower_block, previous[:, :extent])
    moved = source - combine_blocks(lower_block, previous[:, extent:])
    return solve_small(schur, jnp.concatenate([upper_block, moved], 1))


def back_substitute(factors, extent):

    def retreat(following, factor):
        current = factor[:, extent:] - combine_blocks(factor[:, :extent], following)
        return (current, current)

    initial = jnp.zeros(
        (factors.shape[1], factors.shape[2] - extent, factors.shape[3]), jnp.float32
    )
    _, values = lax.scan(retreat, initial, factors, reverse=True)
    return values


def local_factor(viscous, jacobian, source):
    cell_count = viscous.shape[0]
    line_count = viscous.shape[1]

    def advance(previous, inputs):
        vis_cell, jac_cell, src_cell, position = inputs
        lower_block, center_block, upper_block = cell_blocks(vis_cell, jac_cell)
        first_mask = (position == 0).astype(jnp.float32)
        last_mask = (position == cell_count - 1).astype(jnp.float32)
        columns = jnp.concatenate([src_cell, lower_block * first_mask, upper_block * last_mask], 1)
        result = eliminate(previous, lower_block, center_block, upper_block, columns)
        return (result, result)

    initial = jnp.zeros((5, 16, line_count), jnp.float32)
    _, factors = lax.scan(
        advance, initial, (viscous, jacobian, source, jnp.arange(cell_count, dtype=jnp.int32))
    )
    return factors


def reduced_blocks(head_rows, tail_rows):
    empty_block = jnp.zeros_like(head_rows[:, 1:6])
    coupling_prev = jnp.concatenate(
        [
            jnp.concatenate([empty_block, head_rows[:, 1:6]], 1),
            jnp.concatenate([empty_block, tail_rows[:, 1:6]], 1),
        ],
        0,
    )
    coupling_next = jnp.concatenate(
        [
            jnp.concatenate([head_rows[:, 6:11], empty_block], 1),
            jnp.concatenate([tail_rows[:, 6:11], empty_block], 1),
        ],
        0,
    )
    local_part = jnp.concatenate([head_rows[:, 0:1], tail_rows[:, 0:1]], 0)
    diagonal = jnp.eye(10, dtype=jnp.float32)[:, :, None] + jnp.zeros(
        (1, 1, head_rows.shape[2]), jnp.float32
    )
    return (coupling_prev, diagonal, coupling_next, local_part)


def per_device(flux_x, flux_z, viscous, jacobian):
    stream = padded(flux_x, (("line", 0),), 1)
    across = padded(flux_z, (("plane", 2),), 1)
    source = -0.5 * courant * (stream[2:] - stream[:-2]) - 0.5 * courant * (
        across[:, :, 2:] - across[:, :, :-2]
    )
    factors = local_factor(viscous, jacobian, source[:, :, None, :])
    solved = back_substitute(factors, 5)
    head_rows = solved[0]
    tail_rows = solved[-1]
    line_count = viscous.shape[1]
    partitions = lax.axis_size("line")
    coupling_prev, diagonal, coupling_next, local_part = reduced_blocks(head_rows, tail_rows)

    def forward_turn(iteration, mine):
        arrived = from_behind(mine, "line", 1)
        return eliminate(arrived, coupling_prev, diagonal, coupling_next, local_part)

    state = lax.fori_loop(0, partitions, forward_turn, jnp.zeros((10, 11, line_count), jnp.float32))

    def backward_turn(iteration, mine):
        arrived = from_behind(mine, "line", -1)
        return state[:, 10:] - combine_blocks(state[:, :10], arrived)

    ends = lax.fori_loop(0, partitions, backward_turn, jnp.zeros((10, 1, line_count), jnp.float32))
    before = from_behind(ends[5:], "line", 1)
    after = from_behind(ends[:5], "line", -1)
    delta = (
        solved[:, :, 0]
        - jnp.sum(solved[:, :, 1:6] * before[:, 0][None, None], axis=2)
        - jnp.sum(solved[:, :, 6:11] * after[:, 0][None, None], axis=2)
    )
    return delta


def solution(mesh):
    placed = (
        P("line", None, "plane"),
        P("line", None, "plane"),
        P("line", "plane"),
        P("line", None, None, "plane"),
    )
    return jax.shard_map(
        per_device, mesh=mesh, in_specs=placed, out_specs=P("line", None, "plane"), check_vma=False
    )
```

profile of v0, /device:TPU:0, one launch (start us, length us, event | category | flops | bytes accessed | tf_op | source)
XLA Modules:
  0.0 745.2 jit_solution(17539217142998077312)
XLA Ops:
  2.4 3.0 collective-permute-start.5
  7.8 5.5 collective-permute-start.3
  14.7 3.4 fusion.69
  18.2 417.5 %while.85 = (s32[]{:T(128)}, f32[5,16,1024]{2,1,0:T(8,128)S(1)}, f32[64,5,16,1024]{3,2,1,0:T(8,128)}, f32[64,1024]{1,0:T(8,128)}, f32[64,5,5,1024]{3,0,2,1:T(8,1...) while((s32[]{:T(128)}, f32[5,16,1024]{2,1,0:T(8,128)S(1)}, ...), condition=%wide.region_3.4_spmd, body=%wide.region_0.3_spmd.sunk | while | flops 2488376 | bytes 11473969 | solution.py:89
  435.7 9.8 %broadcast_in_dim.31 = f32[64,5,11,1024]{3,2,1,0:T(8,128)} broadcast(f32[]{:T(128)} %constant.952.clone.1), dimensions={} | broadcast | bytes 14417924 | tf_op jit(solution)/shard_map/broadcast_in_dim | solution.py:71
  445.5 129.4 %while.87 = (s32[]{:T(128)}, f32[5,11,1024]{2,1,0:T(8,128)S(1)}, f32[64,5,11,1024]{3,2,1,0:T(8,128)}, f32[64,5,16,1024]{3,2,1,0:T(8,128)}, s32[]{:T(128)}, /*index=5*/s32[]{:T(128)}, s32[]{:T(128)}) while((s32[]{:T(128)}, f32[5,11,1024]{2,1,0:T(8,128)S(1)}, f32[64,5,11,1024]{3,2,1,0:T(8,128)}, f32[64,5,16,1024]{3,2,1,0:T(8,128)}, ...), condition=%wide.region_6.7_spmd.clone, body=%wide.region_4.6_spmd.clone.sunk | while | flops 619524 | bytes 2867307 | solution.py:71
  576.4 89.0 %while.86 = (s32[]{:T(128)}, f32[10,11,1024]{2,1,0:T(8,128)S(1)}, f32[10,10,1024]{2,1,0:T(8,128)S(1)}, f32[10,1,1024]{2,1,0:T(1,128)S(1)}, f32[10,10,1024]{2,1,0:T(8,128)S(1)}, /*index=5*/f32[10,10]{1,0:T(8,128)S(1)}, s32[]{:T(128)}) while((s32[]{:T(128)}, f32[10,11,1024]{2,1,0:T(8,128)S(1)}, f32[10,10,1024]{2,1,0:T(8,128)S(1)}, ...), condition=%wide.region_10.11_spmd.clone, body=%wide.region_7.10_spmd.clone.sunk | while | flops 6903810 | bytes 29651460 | solution.py:136
  576.4 4.9 collective-permute-start
  581.3 14.2 %collective-permute-done = f32[10,11,1024]{2,1,0:T(8,128)S(1)} collective-permute-done((f32[10,11,1024]{2,1,0:T(8,128)S(1)}, f32[10,11,1024]{2,1,0:T(8,128)S(1)}, u32[]{:S(2)}, u32[]{:S(2)}) %collective-permute-start) | collective-permute-done | bytes 450592 | tf_op jit(solution)/shard_map/while/body/eval_jaxpr/ppermute | solution.py:25
  599.6 5.3 collective-permute-start
  605.0 13.3 %collective-permute-done = f32[10,11,1024]{2,1,0:T(8,128)S(1)} collective-permute-done((f32[10,11,1024]{2,1,0:T(8,128)S(1)}, f32[10,11,1024]{2,1,0:T(8,128)S(1)}, u32[]{:S(2)}, u32[]{:S(2)}) %collective-permute-start) | collective-permute-done | bytes 450592 | tf_op jit(solution)/shard_map/while/body/eval_jaxpr/ppermute | solution.py:25
  622.5 5.3 collective-permute-start
  627.8 12.4 %collective-permute-done = f32[10,11,1024]{2,1,0:T(8,128)S(1)} collective-permute-done((f32[10,11,1024]{2,1,0:T(8,128)S(1)}, f32[10,11,1024]{2,1,0:T(8,128)S(1)}, u32[]{:S(2)}, u32[]{:S(2)}) %collective-permute-start) | collective-permute-done | bytes 450592 | tf_op jit(solution)/shard_map/while/body/eval_jaxpr/ppermute | solution.py:25
  644.4 5.3 collective-permute-start
  649.7 11.5 %collective-permute-done = f32[10,11,1024]{2,1,0:T(8,128)S(1)} collective-permute-done((f32[10,11,1024]{2,1,0:T(8,128)S(1)}, f32[10,11,1024]{2,1,0:T(8,128)S(1)}, u32[]{:S(2)}, u32[]{:S(2)}) %collective-permute-start) | collective-permute-done | bytes 450592 | tf_op jit(solution)/shard_map/while/body/eval_jaxpr/ppermute | solution.py:25
  665.4 29.2 %while.88 = (s32[]{:T(128)}, f32[10,1,1024]{2,1,0:T(1,128)S(1)}, f32[10,11,1024]{2,1,0:T(8,128)S(1)}, s32[]{:T(128)}, s32[]{:T(128)}) while((s32[]{:T(128)}, f32[10,1,1024]{2,1,0:T(1,128)S(1)}, f32[10,11,1024]{2,1,0:T(8,128)S(1)}, s32[]{:T(128)}, s32[]{:T(128)}) %tuple.254), condition=%wide.region_13.14_spmd.clone, body=%wide.region_11.13_spmd.clone.sunk | while | flops 215043 | bytes 942191 | solution.py:142
  666.7 6.0 collective-permute-done.1
  674.3 6.0 collective-permute-done.1
  681.8 5.6 collective-permute-done.1
  689.0 5.4 collective-permute-done.1
  695.9 5.8 collective-permute-start.6
  701.8 20.8 %copy.24 = f32[64,5,11,1024]{3,1,0,2:T(8,128)} copy(f32[64,5,11,1024]{3,2,1,0:T(8,128)} %get-tuple-element.701) | data formatting | bytes 28835840 | tf_op jit(solution)/shard_map/while | solution.py:71
  722.7 18.5 %multiply_reduce_fusion.7 = (f32[64,5,1024]{2,1,0:T(8,128)S(1)}, f32[64,5,1024]{2,1,0:T(8,128)S(1)}) fusion(f32[64,5,11,1024]{3,2,1,0:T(8,128)} %get-tuple-element.701, f32[5,1024]{1,0:T(8,128)S(1)} %bitcast.396, f32[5,1024]{1,0:T(8,128)S(1)} %bitcast.395), kind=kLoop, calls=%fused_computation.183 | loop fusion | flops 5898240 | bytes 15769600 | tf_op jit(solution)/shard_map/reduce_sum | solution.py:147
  741.2 2.3 fusion.65
  (4257 shorter events, 465.4 us)
Async XLA Ops:
  1.1 12.2 %collective-permute-start.4 = (f32[64,5,1]{2,0,1:T(8,128)S(1)}, f32[64,5,1]{2,0,1:T(8,128)S(1)}, u32[]{:S(2)}, u32[]{:S(2)}) collective-permute-start(f32[64,5,1]{2,0,1:T(8,128)S(1)} %get-tuple-element.830), channel_id=1, source_target_pairs={{1,0},{2,1},{3,2},{4,3},{5,4},{6,5},{7,6},{9,8},{10,9},{11,10},{12... | collective-permute-start | bytes 3848 | tf_op jit(solution)/shard_map/ppermute | solution.py:17
  2.4 10.9 %collective-permute-start.5 = (f32[64,5,1]{2,0,1:T(8,128)S(1)}, f32[64,5,1]{2,0,1:T(8,128)S(1)}, u32[]{:S(2)}, u32[]{:S(2)}) collective-permute-start(f32[64,5,1]{2,0,1:T(8,128)S(1)} %get-tuple-element.831), channel_id=1, source_target_pairs={{0,1},{1,2},{2,3},{3,4},{4,5},{5,6},{6,7},{8,9},{9,10},{10,11},{11... | collective-permute-start | bytes 3848 | tf_op jit(solution)/shard_map/ppermute | solution.py:14
  6.5 6.8 collective-permute-start.2
  7.8 6.9 collective-permute-start.3
  576.4 19.0 %collective-permute-start = (f32[10,11,1024]{2,1,0:T(8,128)S(1)}, f32[10,11,1024]{2,1,0:T(8,128)S(1)}, u32[]{:S(2)}, u32[]{:S(2)}) collective-permute-start(f32[10,11,1024]{2,1,0:T(8,128)S(1)} %get-tuple-element.1043), channel_id=1, source_target_pairs={{0,8},{8,16},{16,24},{1,9},{9,17},{17,25},{2,10},{10,18},{18,26},{... | collective-permute-start | bytes 1351688 | tf_op jit(solution)/shard_map/while/body/eval_jaxpr/ppermute | solution.py:25
  599.6 18.6 %collective-permute-start = (f32[10,11,1024]{2,1,0:T(8,128)S(1)}, f32[10,11,1024]{2,1,0:T(8,128)S(1)}, u32[]{:S(2)}, u32[]{:S(2)}) collective-permute-start(f32[10,11,1024]{2,1,0:T(8,128)S(1)} %get-tuple-element.1043), channel_id=1, source_target_pairs={{0,8},{8,16},{16,24},{1,9},{9,17},{17,25},{2,10},{10,18},{18,26},{... | collective-permute-start | bytes 1351688 | tf_op jit(solution)/shard_map/while/body/eval_jaxpr/ppermute | solution.py:25
  622.5 17.7 %collective-permute-start = (f32[10,11,1024]{2,1,0:T(8,128)S(1)}, f32[10,11,1024]{2,1,0:T(8,128)S(1)}, u32[]{:S(2)}, u32[]{:S(2)}) collective-permute-start(f32[10,11,1024]{2,1,0:T(8,128)S(1)} %get-tuple-element.1043), channel_id=1, source_target_pairs={{0,8},{8,16},{16,24},{1,9},{9,17},{17,25},{2,10},{10,18},{18,26},{... | collective-permute-start | bytes 1351688 | tf_op jit(solution)/shard_map/while/body/eval_jaxpr/ppermute | solution.py:25
  644.4 16.8 %collective-permute-start = (f32[10,11,1024]{2,1,0:T(8,128)S(1)}, f32[10,11,1024]{2,1,0:T(8,128)S(1)}, u32[]{:S(2)}, u32[]{:S(2)}) collective-permute-start(f32[10,11,1024]{2,1,0:T(8,128)S(1)} %get-tuple-element.1043), channel_id=1, source_target_pairs={{0,8},{8,16},{16,24},{1,9},{9,17},{17,25},{2,10},{10,18},{18,26},{... | collective-permute-start | bytes 1351688 | tf_op jit(solution)/shard_map/while/body/eval_jaxpr/ppermute | solution.py:25
  665.4 7.3 collective-permute-start.1
  673.0 7.3 collective-permute-start.1
  680.5 6.9 collective-permute-start.1
  687.7 6.7 collective-permute-start.1
  694.6 28.0 %collective-permute-start.7 = (f32[5,1,1024]{2,1,0:T(1,128)S(1)}, f32[5,1,1024]{2,1,0:T(1,128)S(1)}, u32[]{:S(2)}, u32[]{:S(2)}) collective-permute-start(f32[5,1,1024]{2,1,0:T(1,128)S(1)} %get-tuple-element.836), channel_id=1, source_target_pairs={{8,0},{16,8},{24,16},{9,1},{17,9},{25,17},{10,2},{18,10},{26,18},{... | collective-permute-start | bytes 61448 | tf_op jit(solution)/shard_map/ppermute | solution.py:25
  695.9 26.7 %collective-permute-start.6 = (f32[5,1,1024]{2,1,0:T(1,128)S(1)}, f32[5,1,1024]{2,1,0:T(1,128)S(1)}, u32[]{:S(2)}, u32[]{:S(2)}) collective-permute-start(f32[5,1,1024]{2,1,0:T(1,128)S(1)} %get-tuple-element.837), channel_id=1, source_target_pairs={{0,8},{8,16},{16,24},{1,9},{9,17},{17,25},{2,10},{10,18},{18,26},{... | collective-permute-start | bytes 61448 | tf_op jit(solution)/shard_map/ppermute | solution.py:25
where the time goes:
time: 757 us; the launch traced here: 745 us
  local copies, waits for them, and re-layouts  285 us (38%)
  other arithmetic  225 us (30%)
  loops' own time  115 us (15%)
  waiting for transfers between devices  75.6 us (10%)
  starting transfers between devices  44.2 us (6%)
    dynamic_slice x128, local copies, waits for them, and re-layouts, local_factor(): lax.scan(advance, initial, (viscous, jacobian, source, jnp.arange(cell_co...  120 us
    another operation x1, loops' own time, local_factor(): lax.scan(advance, initial, (viscous, jacobian, source, jnp.arange(cell_co...  111 us
    ppermute x10, waiting for transfers between devices, from_behind(): return lax.ppermute(block, axis, route)  74.2 us
    squeeze x64, local copies, waits for them, and re-layouts, back_substitute(): _, values = lax.scan(retreat, initial, factors, reverse=True)  63.6 us
    dynamic_update_slice x64, other arithmetic, back_substitute(): _, values = lax.scan(retreat, initial, factors, reverse=True)  52.1 us
    add x64, other arithmetic, cell_blocks(): center_block = (1.0 + 2.0 * spread) * identity  49.6 us
    dynamic_update_slice x64, local copies, waits for them, and re-layouts, local_factor(): lax.scan(advance, initial, (viscous, jacobian, source, jnp.arange(cell_co...  48.6 us
    ppermute x10, starting transfers between devices, from_behind(): return lax.ppermute(block, axis, route)  33.1 us

commit v1 on v0

v1 whole, which is shorter than its diff:
```python
import functools
import jax
import jax.numpy as jnp
from jax import lax
from jax.experimental import pallas as pl
from jax.experimental.pallas import tpu as pltpu
from jax.sharding import PartitionSpec as P

courant = 10.0
MESH = pl.DeviceIdType.MESH
GROUPS = ((0, 4), (4, 4), (8, 3))
CHUNKS = 8
UNROLL = 2


def padded(block, axis, dim):
    count = lax.axis_size(axis)
    forward = [(i, i + 1) for i in range(count - 1)]
    backward = [(target, source) for source, target in forward]
    low = lax.ppermute(
        lax.slice_in_dim(block, block.shape[dim] - 1, None, axis=dim), axis, forward
    )
    high = lax.ppermute(lax.slice_in_dim(block, 0, 1, axis=dim), axis, backward)
    return jnp.concatenate([low, block, high], axis=dim)


def product(left, right):
    total = left[:, 0][:, None] * right[0][None]
    for k in range(1, 5):
        total = total + left[:, k][:, None] * right[k][None]
    return total


def apply(left, vector):
    total = left[:, 0] * vector[0][None]
    for k in range(1, 5):
        total = total + left[:, k] * vector[k][None]
    return total


def inverse(rows):
    a = [[rows[r, c] for c in range(5)] for r in range(5)]
    for k in range(5):
        pivot = 1.0 / a[k][k]
        for c in range(5):
            if c != k:
                a[k][c] = a[k][c] * pivot
        for r in range(5):
            if r != k:
                factor = a[r][k]
                for c in range(5):
                    if c != k:
                        a[r][c] = a[r][c] - factor * a[k][c]
                a[r][k] = -factor * pivot
        a[k][k] = pivot
    return jnp.stack([jnp.stack(row) for row in a])


def kernel(
    count, jac_hbm, vis_ref, src_ref, out_ref,
    jac, fac, basis, ends, msg, in_outer, in_mid, x_msg, in_x,
    inv_ref, free_ref, lead, jac_sem, send_sem, recv_sem,
):
    cells = vis_ref.shape[0]
    tile = vis_ref.shape[1:]
    me = lax.axis_index("line")
    half = count // 2
    step = cells // CHUNKS

    def fetch(chunk):
        part = pl.ds(chunk * step, step)
        return pltpu.make_async_copy(jac_hbm.at[part], jac.at[part], jac_sem.at[chunk])

    for chunk in range(CHUNKS):
        fetch(chunk).start()

    barrier = pltpu.get_barrier_semaphore()

    @pl.when(me > 0)
    def _():
        pl.semaphore_signal(barrier, inc=1, device_id={"line": me - 1}, device_id_type=MESH)

    @pl.when(me < count - 1)
    def _():
        pl.semaphore_signal(barrier, inc=1, device_id={"line": me + 1}, device_id_type=MESH)

    def factor_cell(i):
        v = vis_ref[i]
        a = [[jac[i, r, c, :].reshape(tile) for c in range(5)] for r in range(5)]
        for k in range(5):
            a[k][k] = a[k][k] - v
        for k in range(5):
            pivot = 1.0 / a[k][k]
            for r in range(k + 1, 5):
                a[r][k] = a[r][k] * pivot
                for c in range(k + 1, 5):
                    a[r][c] = a[r][c] - a[r][k] * a[k][c]
            a[k][k] = -pivot
            for c in range(k + 1, 5):
                a[k][c] = a[k][c] * pivot
        for r in range(5):
            for c in range(5):
                fac[i, r * 5 + c] = a[r][c]

    def factor_chunk(chunk, _):
        fetch(chunk).wait()

        def body(j, _):
            for u in range(UNROLL):
                factor_cell(chunk * step + j * UNROLL + u)
            return 0

        return lax.fori_loop(0, step // UNROLL, body, 0)

    lax.fori_loop(0, CHUNKS, factor_chunk, 0)

    def march(first, width):
        has_source = first + width == 11

        def start(low):
            return [
                jnp.stack([
                    jnp.full(tile, 1.0 if first + c == low + r else 0.0, jnp.float32)
                    for c in range(width)
                ])
                for r in range(5)
            ]

        def body(i, state):
            x, d = list(state[:5]), list(state[5:])
            twice = (vis_ref[i] * 2.0)[None]
            w = []
            for r in range(5):
                x[r] = x[r] + d[r]
                basis[i, r, pl.ds(first, width)] = x[r]
                w.append(x[r] + twice * d[r])
            if has_source:
                w = [
                    jnp.concatenate([w[r][: width - 1], w[r][width - 1:] - src_ref[i, r][None]], 0)
                    for r in range(5)
                ]
            f = [[fac[i, r * 5 + c][None] for c in range(5)] for r in range(5)]
            for r in range(1, 5):
                for c in range(r):
                    w[r] = w[r] - f[r][c] * w[c]
            for r in range(4, -1, -1):
                w[r] = w[r] * f[r][r]
                for c in range(r + 1, 5):
                    w[r] = w[r] - f[r][c] * w[c]
            d = [w[r] - d[r] for r in range(5)]
            return (*x, *d)

        state = lax.fori_loop(0, cells, body, (*start(0), *start(5)))
        for r in range(10):
            ends[r, pl.ds(first, width)] = state[r]

    for first, width in GROUPS:
        march(first, width)

    pl.semaphore_wait(barrier, (me > 0).astype(jnp.int32) + (me < count - 1).astype(jnp.int32))

    t11, t12 = lambda: ends[0:5, 0:5], lambda: ends[0:5, 5:10]
    t21, t22 = lambda: ends[5:10, 0:5], lambda: ends[5:10, 5:10]
    t1, t2 = lambda: ends[0:5, 10], lambda: ends[5:10, 10]

    def send_relation(target, place, slot):
        return pltpu.make_async_remote_copy(
            src_ref=msg, dst_ref=place, send_sem=send_sem.at[0], recv_sem=recv_sem.at[slot],
            device_id={"line": target}, device_id_type=MESH,
        )

    def send_x(target):
        return pltpu.make_async_remote_copy(
            src_ref=x_msg, dst_ref=in_x, send_sem=send_sem.at[1], recv_sem=recv_sem.at[2],
            device_id={"line": target}, device_id_type=MESH,
        )

    @pl.when((me > 0) & (me < count - 1))
    def _():
        send_relation(me, in_outer, 0).wait_recv()

    @pl.when(me < half)
    def _():
        @pl.when(me == 0)
        def _():
            lead[0:5, 0:5] = t12()
            lead[5:10, 0:5] = t22()
            lead[0:5, 5] = t1()
            lead[5:10, 5] = t2()

        @pl.when(me > 0)
        def _():
            q = in_outer[:, 0:6]
            lead[0:5, 0:6] = product(t12(), q)
            lead[5:10, 0:6] = product(t22(), q)
            lead[:, 0:5] = lead[:, 0:5] + ends[:, 0:5]
            lead[:, 5] = lead[:, 5] + ends[:, 10]

        inv = inverse(lead[0:5, 0:5])
        inv_ref[...] = inv
        q = product(lead[5:10, 0:5], inv)
        msg[:, 0:5] = q
        msg[:, 5] = lead[5:10, 5] - apply(q, lead[0:5, 5])

    @pl.when(me >= half)
    def _():
        @pl.when(me == count - 1)
        def _():
            free_ref[...] = t12() + t22()
            lead[0:5, 0:5] = -(t11() + t21())
            lead[0:5, 5] = -(t1() + t2())

        @pl.when(me < count - 1)
        def _():
            q = in_outer[:, 0:5]
            free_ref[...] = t22() - product(q, t12())
            lead[0:5, 0:5] = product(q, t11()) - t21()
            lead[0:5, 5] = apply(q, t1()) + in_outer[:, 5] - t2()

        msg[...] = product(inverse(free_ref[...]), lead[0:5, 0:6])

    @pl.when(me < half - 1)
    def _():
        send_relation(me + 1, in_outer, 0).start()

    @pl.when(me == half - 1)
    def _():
        send_relation(me + 1, in_mid, 1).start()

    @pl.when(me == half)
    def _():
        send_relation(me - 1, in_mid, 1).start()

    @pl.when(me > half)
    def _():
        send_relation(me - 1, in_outer, 0).start()

    middle = (me == half - 1) | (me == half)

    @pl.when(middle)
    def _():
        send_relation(me, in_mid, 1).wait_recv()
        gap = msg[...] - in_mid[...]
        in_x[...] = -apply(inverse(gap[:, 0:5]), gap[:, 5])

    @pl.when(jnp.logical_not(middle))
    def _():
        send_x(me).wait_recv()

    @pl.when(me < half)
    def _():
        found = apply(inv_ref[...], in_x[...] - lead[0:5, 5])

        @pl.when(me == 0)
        def _():
            lead[0:5, 6] = jnp.zeros((5,) + tile, jnp.float32)
            lead[5:10, 6] = found

        @pl.when(me > 0)
        def _():
            x_msg[...] = found
            send_x(me - 1).start()
            lead[0:5, 6] = found
            lead[5:10, 6] = apply(in_outer[:, 0:5], found) + in_outer[:, 5]

    @pl.when(me >= half)
    def _():
        x = in_x[...]
        d = apply(msg[:, 0:5], x) + msg[:, 5]
        lead[0:5, 6] = x
        lead[5:10, 6] = d

        @pl.when(me < count - 1)
        def _():
            x_msg[...] = apply(t11(), x) + apply(t12(), d) + t1()
            send_x(me + 1).start()

    z = [lead[k, 6] for k in range(10)]

    def finish(i, _):
        for r in range(5):
            terms = [basis[i, r, k] * z[k] for k in range(10)] + [basis[i, r, 10]]
            while len(terms) > 1:
                terms = [sum(terms[k + 1:k + 2], terms[k]) for k in range(0, len(terms), 2)]
            out_ref[i, r] = terms[0]
        return 0

    lax.fori_loop(0, cells, finish, 0)

    send_relation(me, in_outer, 0).wait_send()

    @pl.when((me > 0) & (me < count - 1))
    def _():
        send_x(me).wait_send()


def per_device(flux_x, flux_z, viscous, jacobian):
    stream = padded(flux_x, "line", 0)
    across = padded(flux_z, "plane", 2)
    source = -0.5 * courant * (stream[2:] - stream[:-2]) - 0.5 * courant * (
        across[:, :, 2:] - across[:, :, :-2]
    )
    cells, lines = viscous.shape
    tile = (lines // 128, 128)
    count = lax.axis_size("line")
    f32 = jnp.float32
    vmem = pl.BlockSpec(memory_space=pltpu.VMEM)
    delta = pl.pallas_call(
        functools.partial(kernel, count),
        out_shape=jax.ShapeDtypeStruct((cells, 5) + tile, f32),
        in_specs=[pl.BlockSpec(memory_space=pl.ANY), vmem, vmem],
        out_specs=vmem,
        scratch_shapes=[
            pltpu.VMEM((cells, 5, 5, lines), f32),
            pltpu.VMEM((cells, 25) + tile, f32),
            pltpu.VMEM((cells, 5, 11) + tile, f32),
            pltpu.VMEM((10, 11) + tile, f32),
            pltpu.VMEM((5, 6) + tile, f32),
            pltpu.VMEM((5, 6) + tile, f32),
            pltpu.VMEM((5, 6) + tile, f32),
            pltpu.VMEM((5,) + tile, f32),
            pltpu.VMEM((5,) + tile, f32),
            pltpu.VMEM((5, 5) + tile, f32),
            pltpu.VMEM((5, 5) + tile, f32),
            pltpu.VMEM((10, 7) + tile, f32),
            pltpu.SemaphoreType.DMA((CHUNKS,)),
            pltpu.SemaphoreType.DMA((2,)),
            pltpu.SemaphoreType.DMA((3,)),
        ],
        compiler_params=pltpu.CompilerParams(
            collective_id=0, has_side_effects=True, vmem_limit_bytes=56 * 1024 * 1024
        ),
    )(jacobian, viscous.reshape((cells,) + tile), source.reshape((cells, 5) + tile))
    return delta.reshape(cells, 5, lines)


def solution(mesh):
    placed = (
        P("line", None, "plane"),
        P("line", None, "plane"),
        P("line", "plane"),
        P("line", None, None, "plane"),
    )
    return jax.shard_map(
        per_device, mesh=mesh, in_specs=placed, out_specs=P("line", None, "plane"), check_vma=False
    )
```

time: 757 us -> 60.5 us (0.08); the launches traced: 745 us -> 60.2 us
  local copies, waits for them, and re-layouts: 285 us -> 18.9 us
  other arithmetic: 225 us -> 0.8 us
  loops' own time: 115 us -> 0 us
  waiting for transfers between devices: 75.6 us -> 0.01 us
  starting transfers between devices: 44.2 us -> 11.1 us
  Pallas kernels: 0 us -> 29.3 us
    dynamic_slice x128 -> x0, local copies, waits for them, and re-layouts: 120 us -> none  [local_factor(): lax.scan(advance, initial, (viscous, jacobian, source, jnp.arange(cell_co...]
    another operation x4 -> x0, loops' own time: 115 us -> none  [the longest x1 111 us: local_factor(): lax.scan(advance, initial, (viscous, jacobian, source, jnp.arange(cell_co...]
    ppermute x14 -> x4, waiting for transfers between devices: 75.6 us -> 0.01 us  [the longest x2 0.01 us: padded(): high = lax.ppermute(lax.slice_in_dim(block, 0, 1, axis=dim), axis, backward)]
    squeeze x129 -> x0, local copies, waits for them, and re-layouts: 66.3 us -> none  [the longest x64 63.6 us: back_substitute(): _, values = lax.scan(retreat, initial, factors, reverse=True)]
    dynamic_update_slice x64 -> x0, other arithmetic: 52.1 us -> none  [back_substitute(): _, values = lax.scan(retreat, initial, factors, reverse=True)]
    add x64 -> x0, other arithmetic: 49.6 us -> none  [cell_blocks(): center_block = (1.0 + 2.0 * spread) * identity]
    dynamic_update_slice x64 -> x0, local copies, waits for them, and re-layouts: 48.6 us -> none  [local_factor(): lax.scan(advance, initial, (viscous, jacobian, source, jnp.arange(cell_co...]
    reduce_sum x205 -> x0, other arithmetic: 46.3 us -> none  [the longest x204 27.8 us: combine_blocks(): return jnp.sum(matrix[:, :, None, :] * operand[None, :, :, :], axis=1)]
where the time goes in v1:
time: 60.5 us; the launch traced here: 60.2 us
  Pallas kernels  29.3 us (48%)
  local copies, waits for them, and re-layouts  18.9 us (31%)
  starting transfers between devices  11.1 us (18%)
  other arithmetic  0.8 us (1%)
    pallas_call x1, Pallas kernels, per_device(): pl.pallas_call(functools.partial(kernel, count), out_shape=jax.ShapeDtype...  29.3 us
    unnamed x7, local copies, waits for them, and re-layouts  13 us
    ppermute x2, starting transfers between devices, padded(): lax.ppermute(lax.slice_in_dim(block, block.shape[dim] - 1, None, axis=dim...  8.51 us
    ppermute x2, starting transfers between devices, padded(): high = lax.ppermute(lax.slice_in_dim(block, 0, 1, axis=dim), axis, backward)  2.58 us
    slice x2, local copies, waits for them, and re-layouts, padded(): high = lax.ppermute(lax.slice_in_dim(block, 0, 1, axis=dim), axis, backward)  2.12 us
    pallas_call x1, local copies, waits for them, and re-layouts, per_device(): pl.pallas_call(functools.partial(kernel, count), out_shape=jax.ShapeDtype...  1.4 us
    reshape x1, local copies, waits for them, and re-layouts, per_device(): return delta.reshape(cells, 5, lines)  1.25 us
  transfers between devices with their start and end apart: 4, of which 0 were waited for; matrix products, arithmetic and copies ran while one was open for 23% of the time, Pallas kernels for 0%

profile of v1, /device:TPU:0, one launch (start us, length us, event | category | flops | bytes accessed | tf_op | source)
XLA Modules:
  0.0 60.2 jit_solution(6092763418218843261)
XLA Ops:
  0.0 1.0 %fusion.5 = (f32[1,5,1024]{2,0,1:T(1,128)S(1)}, f32[1,5,1024]{2,0,1:T(1,128)S(1)}) fusion(f32[64,5,1024]{2,0,1:T(8,128)} %param.4), kind=kLoop, calls=%fused_computation.9 | loop fusion | bytes 81920 | tf_op jit(solution)/shard_map/slice | solution.py:23
  1.0 1.3 %collective-permute-start = (f32[1,5,1024]{2,0,1:T(1,128)S(1)}, f32[1,5,1024]{2,0,1:T(1,128)S(1)}, u32[]{:S(2)}, u32[]{:S(2)}) collective-permute-start(f32[1,5,1024]{2,0,1:T(1,128)S(1)} %get-tuple-element.5), channel_id=1, source_target_pairs={{8,0},{16,8},{24,16},{9,1},{17,9},{25,17},{10,2},{18,10},{26,18},{... | collective-permute-start | bytes 61448 | tf_op jit(solution)/shard_map/ppermute | solution.py:23
  2.3 5.5 %collective-permute-start.1 = (f32[1,5,1024]{2,0,1:T(1,128)S(1)}, f32[1,5,1024]{2,0,1:T(1,128)S(1)}, u32[]{:S(2)}, u32[]{:S(2)}) collective-permute-start(f32[1,5,1024]{2,0,1:T(1,128)S(1)} %get-tuple-element.6), channel_id=1, source_target_pairs={{0,8},{8,16},{16,24},{1,9},{9,17},{17,25},{2,10},{10,18},{18,26},{... | collective-permute-start | bytes 61448 | tf_op jit(solution)/shard_map/ppermute | solution.py:20
  7.8 1.1 %fusion.6 = (f32[64,5,1]{2,0,1:T(8,128)S(1)}, f32[64,5,1]{2,0,1:T(8,128)S(1)}) fusion(f32[64,5,1024]{2,0,1:T(8,128)} %param.5), kind=kLoop, calls=%fused_computation.10 | loop fusion | bytes 5120 | tf_op jit(solution)/shard_map/slice | solution.py:23
  8.9 1.3 %collective-permute-start.2 = (f32[64,5,1]{2,0,1:T(8,128)S(1)}, f32[64,5,1]{2,0,1:T(8,128)S(1)}, u32[]{:S(2)}, u32[]{:S(2)}) collective-permute-start(f32[64,5,1]{2,0,1:T(8,128)S(1)} %get-tuple-element.7), channel_id=1, source_target_pairs={{1,0},{2,1},{3,2},{4,3},{5,4},{6,5},{7,6},{9,8},{10,9},{11,10},{12... | collective-permute-start | bytes 3848 | tf_op jit(solution)/shard_map/ppermute | solution.py:23
  10.2 3.0 %collective-permute-start.3 = (f32[64,5,1]{2,0,1:T(8,128)S(1)}, f32[64,5,1]{2,0,1:T(8,128)S(1)}, u32[]{:S(2)}, u32[]{:S(2)}) collective-permute-start(f32[64,5,1]{2,0,1:T(8,128)S(1)} %get-tuple-element.8), channel_id=1, source_target_pairs={{0,1},{1,2},{2,3},{3,4},{4,5},{5,6},{6,7},{8,9},{9,10},{10,11},{11... | collective-permute-start | bytes 3848 | tf_op jit(solution)/shard_map/ppermute | solution.py:20
  13.3 1.7 %copy.11 = f32[8,8,8,128]{3,2,1,0:T(8,128)} copy(f32[8,8,8,128]{3,1,2,0:T(8,128)} %bitcast.15) | data formatting | bytes 524288
  14.9 0.0 copy-start
  15.0 0.0 copy-start.1
  15.0 11.0 %copy.8.jac_hbm = f32[64,5,5,1024]{3,2,1,0:T(8,128)} copy(f32[64,5,5,1024]{3,0,2,1:T(8,128)} %param.7) | data formatting | bytes 13107200 | tf_op args[3]
  26.0 0.0 collective-permute-done.2
  26.0 0.0 collective-permute-done.3
  26.0 0.0 collective-permute-done
  26.0 0.0 collective-permute-done.1
  26.0 0.0 copy-done
  26.0 0.0 copy-done.1
  26.0 0.8 %fusion.2 = f32[64,5,1024]{2,0,1:T(8,128)S(1)} fusion(f32[64,5,1024]{2,0,1:T(8,128)S(1)} %copy-done, f32[64,5,1]{2,0,1:T(8,128)S(1)} %collective-permute-done.3, f32[64,5,1]{2,0,1:T(8,128)S(1)} %collective-permute-done.2, f32[64,5,1024]{2,0,1:T(8,128)S(1)} %copy-done.1, f32[1,5,1024]{2,0,1:T(1,128)S(1)} %collective-permute-done.1, ...), kind=kLoop, calls=%fused_computation.3 | loop fusion | flops 2949120 | bytes 3975680 | tf_op jit(solution)/shard_map/sub | solution.py:300
  26.8 0.3 copy.12
  27.1 1.1 %copy.9.src_ref = f32[64,5,8,128]{3,2,1,0:T(8,128)} copy(f32[64,5,8,128]{3,2,0,1:T(8,128)S(1)} %bitcast.13) | data formatting | bytes 2621440 | tf_op jit(solution)/shard_map/reshape | solution.py:333
  28.2 29.3 %shard_map.46 = f32[64,5,8,128]{3,2,1,0:T(8,128)} custom-call(f32[64,5,5,1024]{3,2,1,0:T(8,128)} %copy.8.jac_hbm, f32[64,8,128]{2,1,0:T(8,128)} %bitcast.14, f32[64,5,8,128]{3,2,1,0:T(8,128)} %copy.9.src_ref), custom_call_target="tpu_custom_call" | custom-call | tf_op jit(solution)/shard_map/pallas_call | solution.py:308
  57.5 1.4 %copy.10 = f32[64,5,8,128]{3,2,0,1:T(8,128)S(1)} copy(f32[64,5,8,128]{3,2,1,0:T(8,128)} %shard_map.46) | data formatting | bytes 2621440 | tf_op jit(solution)/shard_map/pallas_call | solution.py:308
  59.0 1.3 %reshape.11 = f32[64,5,1024]{2,0,1:T(8,128)} reshape(f32[64,5,8,128]{3,2,0,1:T(8,128)S(1)} %copy.10) | data formatting | bytes 2621440 | tf_op jit(solution)/shard_map/reshape | solution.py:334
Async XLA Ops:
  1.0 25.0 %collective-permute-start = (f32[1,5,1024]{2,0,1:T(1,128)S(1)}, f32[1,5,1024]{2,0,1:T(1,128)S(1)}, u32[]{:S(2)}, u32[]{:S(2)}) collective-permute-start(f32[1,5,1024]{2,0,1:T(1,128)S(1)} %get-tuple-element.5), channel_id=1, source_target_pairs={{8,0},{16,8},{24,16},{9,1},{17,9},{25,17},{10,2},{18,10},{26,18},{... | collective-permute-start | bytes 61448 | tf_op jit(solution)/shard_map/ppermute | solution.py:23
  2.3 23.7 %collective-permute-start.1 = (f32[1,5,1024]{2,0,1:T(1,128)S(1)}, f32[1,5,1024]{2,0,1:T(1,128)S(1)}, u32[]{:S(2)}, u32[]{:S(2)}) collective-permute-start(f32[1,5,1024]{2,0,1:T(1,128)S(1)} %get-tuple-element.6), channel_id=1, source_target_pairs={{0,8},{8,16},{16,24},{1,9},{9,17},{17,25},{2,10},{10,18},{18,26},{... | collective-permute-start | bytes 61448 | tf_op jit(solution)/shard_map/ppermute | solution.py:20
  8.9 17.1 %collective-permute-start.2 = (f32[64,5,1]{2,0,1:T(8,128)S(1)}, f32[64,5,1]{2,0,1:T(8,128)S(1)}, u32[]{:S(2)}, u32[]{:S(2)}) collective-permute-start(f32[64,5,1]{2,0,1:T(8,128)S(1)} %get-tuple-element.7), channel_id=1, source_target_pairs={{1,0},{2,1},{3,2},{4,3},{5,4},{6,5},{7,6},{9,8},{10,9},{11,10},{12... | collective-permute-start | bytes 3848 | tf_op jit(solution)/shard_map/ppermute | solution.py:23
  10.2 15.8 %collective-permute-start.3 = (f32[64,5,1]{2,0,1:T(8,128)S(1)}, f32[64,5,1]{2,0,1:T(8,128)S(1)}, u32[]{:S(2)}, u32[]{:S(2)}) collective-permute-start(f32[64,5,1]{2,0,1:T(8,128)S(1)} %get-tuple-element.8), channel_id=1, source_target_pairs={{0,1},{1,2},{2,3},{3,4},{4,5},{5,6},{6,7},{8,9},{9,10},{10,11},{11... | collective-permute-start | bytes 3848 | tf_op jit(solution)/shard_map/ppermute | solution.py:20
  14.9 11.0 %copy-start = (f32[64,5,1024]{2,0,1:T(8,128)S(1)}, f32[64,5,1024]{2,0,1:T(8,128)}, u32[]{:S(2)}) copy-start(f32[64,5,1024]{2,0,1:T(8,128)} %param.5) | copy-start | bytes 3932164
  15.0 11.1 %copy-start.1 = (f32[64,5,1024]{2,0,1:T(8,128)S(1)}, f32[64,5,1024]{2,0,1:T(8,128)}, u32[]{:S(2)}) copy-start(f32[64,5,1024]{2,0,1:T(8,128)} %param.4) | copy-start | bytes 3932164

commit v2 on v1

--- a/solution.py
+++ b/solution.py
@@ -9,19 +9,6 @@
 courant = 10.0
 MESH = pl.DeviceIdType.MESH
 GROUPS = ((0, 4), (4, 4), (8, 3))
-CHUNKS = 8
-UNROLL = 2
-
-
-def padded(block, axis, dim):
-    count = lax.axis_size(axis)
-    forward = [(i, i + 1) for i in range(count - 1)]
-    backward = [(target, source) for source, target in forward]
-    low = lax.ppermute(
-        lax.slice_in_dim(block, block.shape[dim] - 1, None, axis=dim), axis, forward
-    )
-    high = lax.ppermute(lax.slice_in_dim(block, 0, 1, axis=dim), axis, backward)
-    return jnp.concatenate([low, block, high], axis=dim)
 
 
 def product(left, right):
@@ -57,62 +44,123 @@
 
 
 def kernel(
-    count, jac_hbm, vis_ref, src_ref, out_ref,
-    jac, fac, basis, ends, msg, in_outer, in_mid, x_msg, in_x,
-    inv_ref, free_ref, lead, jac_sem, send_sem, recv_sem,
+    count, planes, flux_x_hbm, flux_z_hbm, vis_hbm, jac_hbm, out_ref,
+    flux_x, flux_z, vis, jac, x_low, x_high, z_low, z_high, across, twice, src,
+    fac, basis, ends, msg, in_outer, in_mid, x_msg, in_x, inv_ref, free_ref, lead,
+    local_sem, jac_sem, halo_send, halo_recv, send_sem, recv_sem,
 ):
-    cells = vis_ref.shape[0]
-    tile = vis_ref.shape[1:]
-    me = lax.axis_index("line")
+    blocks, rows, lines = vis.shape
+    cells = blocks * rows
+    tile = (lines // 128, 128)
+    me, plane = lax.axis_index("line"), lax.axis_index("plane")
     half = count // 2
-    step = cells // CHUNKS
-
-    def fetch(chunk):
-        part = pl.ds(chunk * step, step)
-        return pltpu.make_async_copy(jac_hbm.at[part], jac.at[part], jac_sem.at[chunk])
-
-    for chunk in range(CHUNKS):
-        fetch(chunk).start()
-
+
+    def fetch(block):
+        return pltpu.make_async_copy(jac_hbm.at[:, :, block], jac.at[:, :, block], jac_sem.at[block])
+
+    fetch_vis = pltpu.make_async_copy(vis_hbm, vis, local_sem.at[0])
+    fetch_x = pltpu.make_async_copy(flux_x_hbm, flux_x, local_sem.at[1])
+    fetch_z = pltpu.make_async_copy(flux_z_hbm, flux_z, local_sem.at[2])
+
+    fetch_vis.start()
+    for block in range(blocks):
+        fetch(block).start()
+    fetch_x.start()
+    fetch_z.start()
+
+    def halo(slot, source, target, where):
+        return pltpu.make_async_remote_copy(
+            src_ref=source, dst_ref=target, send_sem=halo_send.at[slot],
+            recv_sem=halo_recv.at[slot], device_id=where, device_id_type=MESH,
+        )
+
+    halos = (
+        (me < count - 1, me > 0, x_low, halo(0, flux_x_hbm.at[:, blocks - 1], x_low, {"line": me + 1})),
+        (me > 0, me < count - 1, x_high, halo(1, flux_x_hbm.at[:, 0], x_high, {"line": me - 1})),
+        (plane < planes - 1, plane > 0, z_low,
+         halo(2, flux_z_hbm.at[:, :, :, pl.ds(lines - 128, 128)], z_low, {"plane": plane + 1})),
+        (plane > 0, plane < planes - 1, z_high,
+         halo(3, flux_z_hbm.at[:, :, :, pl.ds(0, 128)], z_high, {"plane": plane - 1})),
+    )
     barrier = pltpu.get_barrier_semaphore()
-
-    @pl.when(me > 0)
-    def _():
-        pl.semaphore_signal(barrier, inc=1, device_id={"line": me - 1}, device_id_type=MESH)
-
-    @pl.when(me < count - 1)
-    def _():
-        pl.semaphore_signal(barrier, inc=1, device_id={"line": me + 1}, device_id_type=MESH)
-
-    def factor_cell(i):
-        v = vis_ref[i]
-        a = [[jac[i, r, c, :].reshape(tile) for c in range(5)] for r in range(5)]
-        for k in range(5):
-            a[k][k] = a[k][k] - v
-        for k in range(5):
-            pivot = 1.0 / a[k][k]
-            for r in range(k + 1, 5):
-                a[r][k] = a[r][k] * pivot
+    for sends, receives, buffer, copy in halos:
+
+        @pl.when(sends)
+        def _():
+            pl.semaphore_signal(barrier, inc=1, device_id=copy.device_id, device_id_type=MESH)
+
+        @pl.when(jnp.logical_not(receives))
+        def _():
+            buffer[...] = jnp.zeros_like(buffer)
+
+    pl.semaphore_wait(barrier, sum(sends.astype(jnp.int32) for sends, _, _, _ in halos))
+    for sends, receives, buffer, copy in halos:
+
+        @pl.when(sends)
+        def _():
+            copy.start()
+
+    fetch_vis.wait()
+
+    def factor_block(block, _):
+        fetch(block).wait()
+        for u in range(rows):
+            i = block * rows + u
+            v = vis[block, u, :].reshape(tile)
+            twice[i] = v * 2.0
+            a = [[jac[r, c, block, u, :].reshape(tile) for c in range(5)] for r in range(5)]
+            for k in range(5):
+                a[k][k] = a[k][k] - v
+            for k in range(5):
+                pivot = 1.0 / a[k][k]
+                for r in range(k + 1, 5):
+                    a[r][k] = a[r][k] * pivot
+                    for c in range(k + 1, 5):
+                        a[r][c] = a[r][c] - a[r][k] * a[k][c]
+                a[k][k] = -pivot
                 for c in range(k + 1, 5):
-                    a[r][c] = a[r][c] - a[r][k] * a[k][c]
-            a[k][k] = -pivot
-            for c in range(k + 1, 5):
-                a[k][c] = a[k][c] * pivot
-        for r in range(5):
-            for c in range(5):
-                fac[i, r * 5 + c] = a[r][c]
-
-    def factor_chunk(chunk, _):
-        fetch(chunk).wait()
-
-        def body(j, _):
-            for u in range(UNROLL):
-                factor_cell(chunk * step + j * UNROLL + u)
-            return 0
-
-        return lax.fori_loop(0, step // UNROLL, body, 0)
-
-    lax.fori_loop(0, CHUNKS, factor_chunk, 0)
+                    a[k][c] = a[k][c] * pivot
+            for r in range(5):
+                for c in range(5):
+                    fac[i, r * 5 + c] = a[r][c]
+        return 0
+
+    lax.fori_loop(0, blocks, factor_block, 0)
+
+    def make_source():
+        fetch_x.wait()
+        fetch_z.wait()
+        for sends, receives, buffer, copy in halos:
+
+            @pl.when(receives)
+            def _():
+                copy.wait_recv()
+
+        lane = lax.broadcasted_iota(jnp.int32, (rows, 128), 1)
+
+        def body(block, before):
+            now = []
+            for r in range(5):
+                middle = flux_z[r, block]
+                up = pltpu.roll(middle, lines - 1, 1)
+                down = pltpu.roll(middle, 1, 1)
+                first = jnp.where(lane == 0, pltpu.roll(z_low[r, block], 1, 1), down[:, :128])
+                last = jnp.where(lane == 127, pltpu.roll(z_high[r, block], 127, 1), up[:, lines - 128:])
+                up = jnp.concatenate([up[:, : lines - 128], last], 1)
+                down = jnp.concatenate([first, down[:, 128:]], 1)
+                across[r] = up - down
+                here = [flux_x[r, block, u, :].reshape(tile) for u in range(rows)]
+                following = flux_x[r, jnp.minimum(block + 1, blocks - 1), 0, :].reshape(tile)
+                following = jnp.where(block == blocks - 1, x_high[r, 0, :].reshape(tile), following)
+                stream = [before[r]] + here + [following]
+                now.append(here[-1])
+                for u in range(rows):
+                    src[block * rows + u, r] = (-0.5 * courant) * (stream[u + 2] - stream[u]) + (
+                        -0.5 * courant
+                    ) * across[r, u, :].reshape(tile)
+            return tuple(now)
+
+        lax.fori_loop(0, blocks, body, tuple(x_low[r, rows - 1, :].reshape(tile) for r in range(5)))
 
     def march(first, width):
         has_source = first + width == 11
@@ -128,15 +176,15 @@
 
         def body(i, state):
             x, d = list(state[:5]), list(state[5:])
-            twice = (vis_ref[i] * 2.0)[None]
+            two = twice[i][None]
             w = []
             for r in range(5):
                 x[r] = x[r] + d[r]
                 basis[i, r, pl.ds(first, width)] = x[r]
-                w.append(x[r] + twice * d[r])
+                w.append(x[r] + two * d[r])
             if has_source:
                 w = [
-                    jnp.concatenate([w[r][: width - 1], w[r][width - 1:] - src_ref[i, r][None]], 0)
+                    jnp.concatenate([w[r][: width - 1], w[r][width - 1:] - src[i, r][None]], 0)
                     for r in range(5)
                 ]
             f = [[fac[i, r * 5 + c][None] for c in range(5)] for r in range(5)]
@@ -155,9 +203,9 @@
             ends[r, pl.ds(first, width)] = state[r]
 
     for first, width in GROUPS:
+        if first + width == 11:
+            make_source()
         march(first, width)
-
-    pl.semaphore_wait(barrier, (me > 0).astype(jnp.int32) + (me < count - 1).astype(jnp.int32))
 
     t11, t12 = lambda: ends[0:5, 0:5], lambda: ends[0:5, 5:10]
     t21, t22 = lambda: ends[5:10, 0:5], lambda: ends[5:10, 5:10]
@@ -277,15 +325,23 @@
 
     z = [lead[k, 6] for k in range(10)]
 
-    def finish(i, _):
-        for r in range(5):
-            terms = [basis[i, r, k] * z[k] for k in range(10)] + [basis[i, r, 10]]
-            while len(terms) > 1:
-                terms = [sum(terms[k + 1:k + 2], terms[k]) for k in range(0, len(terms), 2)]
-            out_ref[i, r] = terms[0]
+    def finish(block, _):
+        for u in range(rows):
+            i = block * rows + u
+            for r in range(5):
+                terms = [basis[i, r, k] * z[k] for k in range(10)] + [basis[i, r, 10]]
+                while len(terms) > 1:
+                    terms = [sum(terms[k + 1:k + 2], terms[k]) for k in range(0, len(terms), 2)]
+                out_ref[r, block, u, :] = terms[0].reshape(lines)
         return 0
 
-    lax.fori_loop(0, cells, finish, 0)
+    lax.fori_loop(0, blocks, finish, 0)
+
+    for sends, receives, buffer, copy in halos:
+
+        @pl.when(sends)
+        def _():
+            copy.wait_send()
 
     send_relation(me, in_outer, 0).wait_send()
 
@@ -295,23 +351,29 @@
 
 
 def per_device(flux_x, flux_z, viscous, jacobian):
-    stream = padded(flux_x, "line", 0)
-    across = padded(flux_z, "plane", 2)
-    source = -0.5 * courant * (stream[2:] - stream[:-2]) - 0.5 * courant * (
-        across[:, :, 2:] - across[:, :, :-2]
-    )
     cells, lines = viscous.shape
+    rows = 8
+    blocks = cells // rows
     tile = (lines // 128, 128)
-    count = lax.axis_size("line")
     f32 = jnp.float32
-    vmem = pl.BlockSpec(memory_space=pltpu.VMEM)
+    line_cells = (blocks, rows, lines)
     delta = pl.pallas_call(
-        functools.partial(kernel, count),
-        out_shape=jax.ShapeDtypeStruct((cells, 5) + tile, f32),
-        in_specs=[pl.BlockSpec(memory_space=pl.ANY), vmem, vmem],
-        out_specs=vmem,
+        functools.partial(kernel, lax.axis_size("line"), lax.axis_size("plane")),
+        out_shape=jax.ShapeDtypeStruct((5,) + line_cells, f32),
+        in_specs=[pl.BlockSpec(memory_space=pl.ANY)] * 4,
+        out_specs=pl.BlockSpec(memory_space=pltpu.VMEM),
         scratch_shapes=[
-            pltpu.VMEM((cells, 5, 5, lines), f32),
+            pltpu.VMEM((5,) + line_cells, f32),
+            pltpu.VMEM((5,) + line_cells, f32),
+            pltpu.VMEM(line_cells, f32),
+            pltpu.VMEM((5, 5) + line_cells, f32),
+            pltpu.VMEM((5, rows, lines), f32),
+            pltpu.VMEM((5, rows, lines), f32),
+            pltpu.VMEM((5, blocks, rows, 128), f32),
+            pltpu.VMEM((5, blocks, rows, 128), f32),
+            pltpu.VMEM((5, rows, lines), f32),
+            pltpu.VMEM((cells,) + tile, f32),
+            pltpu.VMEM((cells, 5) + tile, f32),
             pltpu.VMEM((cells, 25) + tile, f32),
             pltpu.VMEM((cells, 5, 11) + tile, f32),
             pltpu.VMEM((10, 11) + tile, f32),
@@ -323,15 +385,23 @@
             pltpu.VMEM((5, 5) + tile, f32),
             pltpu.VMEM((5, 5) + tile, f32),
             pltpu.VMEM((10, 7) + tile, f32),
-            pltpu.SemaphoreType.DMA((CHUNKS,)),
+            pltpu.SemaphoreType.DMA((3,)),
+            pltpu.SemaphoreType.DMA((blocks,)),
+            pltpu.SemaphoreType.DMA((4,)),
+            pltpu.SemaphoreType.DMA((4,)),
             pltpu.SemaphoreType.DMA((2,)),
             pltpu.SemaphoreType.DMA((3,)),
         ],
         compiler_params=pltpu.CompilerParams(
             collective_id=0, has_side_effects=True, vmem_limit_bytes=56 * 1024 * 1024
         ),
-    )(jacobian, viscous.reshape((cells,) + tile), source.reshape((cells, 5) + tile))
-    return delta.reshape(cells, 5, lines)
+    )(
+        flux_x.transpose(1, 0, 2).reshape((5,) + line_cells),
+        flux_z.transpose(1, 0, 2).reshape((5,) + line_cells),
+        viscous.reshape(line_cells),
+        jacobian.transpose(1, 2, 0, 3).reshape((5, 5) + line_cells),
+    )
+    return delta.reshape(5, cells, lines).transpose(1, 0, 2)
 
 
 def solution(mesh):

time: 60.5 us -> 32.9 us (0.54)
  local copies, waits for them, and re-layouts: 18.9 us -> 2.52 us
  starting transfers between devices: 11.1 us -> 0 us
  Pallas kernels: 29.3 us -> 30.2 us
  other arithmetic: 0.8 us -> 0 us
    ppermute x4 -> x0, starting transfers between devices: 11.1 us -> none  [the longest x2 8.51 us: padded(): lax.ppermute(lax.slice_in_dim(block, block.shape[dim] - 1, None, axis=dim...]
    unnamed x7 -> x1, local copies, waits for them, and re-layouts: 13 us -> 2.52 us
    reshape x2 -> x0, local copies, waits for them, and re-layouts: 2.4 us -> none  [the longest x1 1.25 us: per_device(): return delta.reshape(cells, 5, lines)]
    slice x2 -> x0, local copies, waits for them, and re-layouts: 2.12 us -> none  [padded(): high = lax.ppermute(lax.slice_in_dim(block, 0, 1, axis=dim), axis, backward)]
    pallas_call x1 -> x0, local copies, waits for them, and re-layouts: 1.4 us -> none  [per_device(): pl.pallas_call(functools.partial(kernel, count), out_shape=jax.ShapeDtype...]
    pallas_call x1, Pallas kernels: 29.3 us -> 30.2 us  [per_device(): pl.pallas_call(functools.partial(kernel, lax.axis_size('line'), lax.axis_...]
    sub x1 -> x0, other arithmetic: 0.8 us -> none  [per_device(): -0.5 * courant * (stream[2:] - stream[:-2])]
  transfers between devices with their start and end apart: 4 -> 0, of which waited for: 0 -> 0; matrix products, arithmetic and copies ran while one was open for 23% -> 0% of each run, Pallas kernels for 0% -> 0%
where the time goes in v2:
time: 32.9 us; the launch traced here: 32.7 us
  Pallas kernels  30.2 us (92%)
  local copies, waits for them, and re-layouts  2.52 us (8%)
    pallas_call x1, Pallas kernels, per_device(): pl.pallas_call(functools.partial(kernel, lax.axis_size('line'), lax.axis_...  30.2 us
    unnamed x1, local copies, waits for them, and re-layouts  2.52 us

profile of v2, /device:TPU:0, one launch (start us, length us, event | category | flops | bytes accessed | tf_op | source)
XLA Modules:
  0.0 32.7 jit_solution(11846069183338938010)
XLA Ops:
  0.0 30.2 %shard_map.46 = f32[5,8,8,1024]{3,2,1,0:T(8,128)} custom-call(f32[5,8,8,1024]{3,2,1,0:T(8,128)} %bitcast.15, f32[5,8,8,1024]{3,2,1,0:T(8,128)} %bitcast.16, f32[8,8,1024]{2,1,0:T(8,128)} %bitcast.17, f32[5,5,8,8,1024]{4,3,2,1,0:T(8,128)} %bitcast.13), custom_call_target="tpu_custom_call" | custom-call | tf_op jit(solution)/shard_map/pallas_call | solution.py:360
  30.2 2.5 %copy.6 = f32[64,5,1024]{2,0,1:T(8,128)} copy(f32[64,5,1024]{2,0,1:T(8,128)} %bitcast.14) | data formatting | bytes 2621440

commit v3 on v2

--- a/solution.py
+++ b/solution.py
@@ -198,7 +198,7 @@
             d = [w[r] - d[r] for r in range(5)]
             return (*x, *d)
 
-        state = lax.fori_loop(0, cells, body, (*start(0), *start(5)))
+        state = lax.fori_loop(0, cells, body, (*start(0), *start(5)), unroll=2)
         for r in range(10):
             ends[r, pl.ds(first, width)] = state[r]
 

time: 32.9 us -> 32.2 us (0.979)
  Pallas kernels: 30.2 us -> 29.5 us
    pallas_call x1, Pallas kernels: 30.2 us -> 29.5 us  [per_device(): pl.pallas_call(functools.partial(kernel, lax.axis_size('line'), lax.axis_...]
where the time goes in v3:
time: 32.2 us; the launch traced here: 32 us
  Pallas kernels  29.5 us (92%)
  local copies, waits for them, and re-layouts  2.52 us (8%)
    pallas_call x1, Pallas kernels, per_device(): pl.pallas_call(functools.partial(kernel, lax.axis_size('line'), lax.axis_...  29.5 us
    unnamed x1, local copies, waits for them, and re-layouts  2.52 us

profile of v3, /device:TPU:0, one launch (start us, length us, event | category | flops | bytes accessed | tf_op | source)
XLA Modules:
  0.0 32.0 jit_solution(2092488457424393399)
XLA Ops:
  0.0 29.5 %shard_map.46 = f32[5,8,8,1024]{3,2,1,0:T(8,128)} custom-call(f32[5,8,8,1024]{3,2,1,0:T(8,128)} %bitcast.15, f32[5,8,8,1024]{3,2,1,0:T(8,128)} %bitcast.16, f32[8,8,1024]{2,1,0:T(8,128)} %bitcast.17, f32[5,5,8,8,1024]{4,3,2,1,0:T(8,128)} %bitcast.13), custom_call_target="tpu_custom_call" | custom-call | tf_op jit(solution)/shard_map/pallas_call | solution.py:360
  29.5 2.5 %copy.6 = f32[64,5,1024]{2,0,1:T(8,128)} copy(f32[64,5,1024]{2,0,1:T(8,128)} %bitcast.14) | data formatting | bytes 2621440
